TPU v7x, 128 devices: a whole 4x4x4 slice. The times are simulated.
128 devices in a mesh: outer: 8 (over y, x_lo), inner: 4 (over z), tensor: 4 (over x_hi, core).
Axes of the slice: x: 4 (x_hi: 2, x_lo: 2; x = x_hi * 2 + x_lo), y: 4, z: 4, core: 2. Of those that a mesh axis runs over, the one named last changes fastest.
Arguments:
- queries: bfloat16 [16384, 4096], P(('outer', 'inner'), 'tensor'), may hold values from -8 to 8
- keys: bfloat16 [16384, 512], P(('outer', 'inner'), 'tensor'), may hold values from -6 to 6
- values: bfloat16 [16384, 512], P(('outer', 'inner'), 'tensor'), may hold values from -6 to 6
- positions: int32 [16384], P(('outer', 'inner')), may hold values from 0 to 16383, as said below
- out_weight: bfloat16 [4096, 4096], P('tensor'), may hold values from -0.5 to 0.5
Outputs:
- projected: bfloat16 [16384, 4096], P(('outer', 'inner'))
Inputs may be any that keep to these rules, and one draw needn't show every extreme that they name: Along outer+inner, each device's 512 stored tokens are two runs of 256 consecutive increasing positions, each run starting at a multiple of 256; every position from 0 to 16383 occurs exactly once.
All inputs are finite; a program needn't handle non-finite values.
Results may differ from a plain program's by a relative error of at most 0.018.
Values may be sent and summed in bfloat16 or wider, within the bound.
No kernel may reach another device: no remote copies, remote signals or barrier semaphores. Data moves between devices by JAX's collectives and lax.ppermute only.
A program may use at most 576 MiB of HBM per device.

v0:
```python
import functools
import math

import jax
import jax.numpy as jnp
import numpy as np
from jax import lax
from jax.experimental import pallas as pl
from jax.experimental.pallas import tpu as pltpu
from jax.sharding import Mesh
from jax.sharding import PartitionSpec as P

D = 128
RUN = 256
AXES = ("y", "xl", "z", "xh", "c")
SIZES = (4, 2, 4, 2, 2)
SCALE = math.log2(math.e) / math.sqrt(D)
ROWS = 528
NQ = 4096
PER = 1024
TILE = 512
UNROLL = 4
LIMIT = 100.0
SHIFTS = (0, 1, 3, 2)
SHARE = 256
SHARE = 256
OWN = (0, 8, 1, 9)
VMEM = 28 * 2**20
PART = 16
PER = 1024
TILE = 512
UNROLL = 4
LIMIT = 100.0
SHIFTS = (0, 1, 3, 2)
SHARE = 256
OWN = (0, 8, 1, 9)
VMEM = 28 * 2**20
F32, BF16, I32 = jnp.float32, jnp.bfloat16, jnp.int32


def route(block, f):
    pairs = [
        (int(np.ravel_multi_index(i, SIZES)), int(np.ravel_multi_index(f(*i), SIZES)))
        for i in np.ndindex(*SIZES)
    ]
    return lax.ppermute(block, AXES, pairs)


def onward(block, d, stage):
    def f(y, xl, z, xh, c):
        return (y, xl, (z + d) % 4, xh, c) if c == stage else ((y + d) % 4, xl, z, xh, c)

    return route(block, f)


def other_core(block):
    return route(block, lambda y, xl, z, xh, c: (y, xl, z, xh, 1 - c))


def values_of(kv, slot):
    ones = kv[slot, 512:528, :]
    return [jnp.concatenate([kv[slot, 256 + 128 * h : 384 + 128 * h, :], ones], axis=0) for h in (0, 1)]


def keys_of(kv, slot):
    return kv[slot, 0:256, :]


def work_list(order, items, ranks, count, rank, run, n):
    def put(s, found):
        order[found] = s
        return found + (ranks[s] < rank).astype(I32)

    found = lax.fori_loop(0, count, put, jnp.int32(0))
    order[found] = count

    def pair(p, n):
        items[0, n] = run
        items[1, n] = order[2 * p]
        items[2, n] = order[2 * p + 1]
        return n + 1

    return lax.fori_loop(0, (found + 1) // 2, pair, n)


def absorb_items(items, n, kv, base, count, qt, mref, acc, viol):
    for u in range(UNROLL):
        items[0, n + u] = 0
        items[1, n + u] = count
        items[2, n + u] = count

    @pl.loop(0, (n + UNROLL - 1) // UNROLL)
    def _(t):
        steps = []
        for u in range(UNROLL):
            run, a, b = (items[w, t * UNROLL + u] for w in range(3))
            a, b = a + base, b + base
            k = jnp.concatenate([keys_of(kv, a), keys_of(kv, b)], axis=0)
            k = jnp.concatenate([k, k], axis=1)
            v = jnp.concatenate(values_of(kv, a) + values_of(kv, b), axis=1)
            steps += [(k, v, run, slice(j * TILE, (j + 1) * TILE)) for j in range(PER // TILE)]

        def score(i):
            k, _, run, cols = steps[i]
            return jnp.dot(k, qt[run, :, cols], preferred_element_type=F32)

        s = score(0)
        for i, (_, v, run, cols) in enumerate(steps):
            later = score(i + 1) if i + 1 < len(steps) else None
            x = s - mref[run, :, cols]
            viol[run, :, cols] = jnp.maximum(viol[run, :, cols], jnp.max(x.reshape(2 * RUN // 8, 8, TILE), axis=0))
            p = jnp.exp2(x).astype(BF16)
            acc[run, :, cols] += jnp.dot(v, p, preferred_element_type=F32)
            s = later


def read_ranks(kv, base, count, ranks):
    for s in range(count):
        ranks[s] = jnp.max(kv[base + s, 512:528, :].astype(F32)).astype(I32)


def fill(kv, base, sources, sems):
    copies = []
    for i, src in enumerate(sources):
        copy = pltpu.make_async_copy(src, kv.at[pl.ds(base, src.shape[0])], sems.at[i])
        copy.start()
        copies.append(copy)
        base += src.shape[0]
    return copies


def set_ones(kv, first, count):
    kv[pl.ds(first, count), 512:528, :] = jnp.ones((count, 16, D), BF16)


def turn_kernel(q0, q1, qt):
    for i in range(4):
        for h in range(4):
            rows = slice(i // 2 * RUN, (i // 2 + 1) * RUN)
            block = (q0, q1)[i % 2][rows, h * D : (h + 1) * D].astype(F32).T * SCALE
            high = block.astype(BF16)
            here = slice(h * RUN, (h + 1) * RUN)
            qt[i, 0:D, here] = high
            qt[i, D : 2 * D, here] = (block - high.astype(F32)).astype(BF16)


def early_kernel(qt, s0, s1, ranks, mref, acc, viol, kv, order, items, sems):
    for copy in fill(kv, 0, (s0, s1), sems):
        copy.wait()
    read_ranks(kv, 0, PART, ranks)
    n = jnp.int32(0)
    for i in range(4):
        n = work_list(order, items, ranks, PART, ranks[OWN[i]], i, n)
    set_ones(kv, 0, PART)
    kv[PART] = jnp.zeros((ROWS, D), BF16)
    key = lax.broadcasted_iota(I32, (RUN, PER), 0)
    query = lax.broadcasted_iota(I32, (RUN, PER), 1) % RUN
    keep = key <= query
    for i in range(4):
        k = keys_of(kv, OWN[i])
        s = jnp.dot(jnp.concatenate([k, k], axis=1), qt[i], preferred_element_type=F32)
        s = jnp.where(keep, s, -1e30)
        top = jnp.max(s, axis=0, keepdims=True)
        mref[i] = top
        p = jnp.exp2(s - top).astype(BF16)
        v = jnp.concatenate(values_of(kv, OWN[i]), axis=1)
        acc[i] = jnp.dot(v, p, preferred_element_type=F32)
    viol[...] = jnp.zeros_like(viol)
    absorb_items(items, n, kv, 0, PART, qt, mref, acc, viol)


def take_state(state, held, first, count, sems):
    copies = []
    for i, (src, dst) in enumerate(zip(state, held)):
        copy = pltpu.make_async_copy(src.at[pl.ds(first, count)], dst, sems.at[i])
        copy.start()
        copies.append(copy)
    return copies


def middle_kernel(early_ranks, qt, mref, acc_in, viol_in, s0, s1, ranks, acc, viol, kv, order, items, sems):
    copies = fill(kv, 0, (s0, s1), sems)
    acc[...] = acc_in[...]
    viol[...] = viol_in[...]
    for copy in copies:
        copy.wait()
    read_ranks(kv, 0, PART, ranks)
    n = jnp.int32(0)
    for i in range(4):
        n = work_list(order, items, ranks, PART, early_ranks[OWN[i]], i, n)
    set_ones(kv, 0, PART)
    kv[PART] = jnp.zeros((ROWS, D), BF16)
    absorb_items(items, n, kv, 0, PART, qt, mref, acc, viol)


def late_kernel(chunk, early_ranks, middle_ranks, *rest):
    state, sources = rest[:4], rest[4:12]
    *out, kv, qt, mref, acc, viol, ranks, order, items, sems, state_sems = rest[12:]
    base, count = 2 * PART, 2 * PART
    copies = fill(kv, base, sources[4:], sems)
    copies += take_state(state, (qt, mref, acc, viol), 2 * chunk, 2, state_sems)
    for copy in copies:
        copy.wait()
    read_ranks(kv, base, count, ranks)
    n = jnp.int32(0)
    for i in range(2):
        n = work_list(order, items, ranks, count, early_ranks[OWN[2 * chunk + i]], i, n)
    set_ones(kv, base, count)
    kv[base + count] = jnp.zeros((ROWS, D), BF16)
    absorb_items(items, n, kv, base, count, qt, mref, acc, viol)

    @pl.when(jnp.max(viol[...]) > LIMIT)
    def _():
        for copy in fill(kv, 0, sources[:4], sems):
            copy.wait()
        set_ones(kv, 0, base)
        later = lax.broadcasted_iota(I32, (RUN, RUN), 0) > lax.broadcasted_iota(I32, (RUN, RUN), 1)

        def take(slot, slot_rank, run, rank, cols):
            @pl.when(slot_rank <= rank)
            def _():
                k = keys_of(kv, slot)
                s = jnp.dot(jnp.concatenate([k, k], axis=1), qt[run, :, cols], preferred_element_type=F32)
                drop = jnp.logical_and(later, jnp.full((RUN, RUN), slot_rank, I32) == rank)
                s = jnp.where(drop, -1e30, s)
                old = viol[run, 0:1, cols]
                top = jnp.maximum(old, jnp.max(s, axis=0, keepdims=True))
                viol[run, 0:1, cols] = top
                p = jnp.exp2(s - top).astype(BF16)
                v = jnp.concatenate(values_of(kv, slot), axis=1)
                term = jnp.dot(v, p, preferred_element_type=F32)
                acc[run, :, cols] = acc[run, :, cols] * jnp.exp2(old - top) + term

        @pl.loop(0, 2 * PER // RUN)
        def _(t):
            run = t // (PER // RUN)
            cols = pl.ds(pl.multiple_of(t % (PER // RUN) * RUN, RUN), RUN)
            rank = jnp.where(run == 0, early_ranks[OWN[2 * chunk]], early_ranks[OWN[2 * chunk + 1]])
            acc[run, :, cols] = jnp.zeros((144, RUN), F32)
            viol[run, :, cols] = jnp.full((8, RUN), -1e30, F32)
            for first, held, many in ((0, early_ranks, PART), (PART, middle_ranks, PART), (base, ranks, count)):

                @pl.loop(0, many)
                def _(s, first=first, held=held):
                    take(first + s, held[s], run, rank, cols)

    for i in range(2):
        for h in range(4):
            cols = slice(h * RUN, (h + 1) * RUN)
            block = acc[i, 0:D, cols] / acc[i, D : D + 1, cols]
            out[i][:, h * D : (h + 1) * D] = block.T.astype(BF16)


def spec(space):
    return pl.BlockSpec(memory_space=space)


def cost(slots, runs):
    pairs = slots * RUN * runs * PER // 2
    return pl.CostEstimate(flops=8 * D * pairs, bytes_accessed=12 * 10**6, transcendentals=pairs)


RANKS = jax.ShapeDtypeStruct((PART,), I32)
def held(runs):
    return [pltpu.VMEM((runs, 2 * D, PER), BF16), pltpu.VMEM((runs, 1, PER), F32)]


STATE = (jax.ShapeDtypeStruct((4, 144, PER), F32), jax.ShapeDtypeStruct((4, 8, PER), F32))
PARAMS = pltpu.CompilerParams(vmem_limit_bytes=VMEM)
LARGE = pltpu.CompilerParams(vmem_limit_bytes=56 * 2**20)
SMALL = pltpu.CompilerParams(vmem_limit_bytes=12 * 2**20)


def lists(slots):
    return [pltpu.SMEM((slots + 8,), I32), pltpu.SMEM((3, 2 * slots + 16), I32)]


def turn(q0, q1):
    return pl.pallas_call(
        turn_kernel,
        name="turn_queries",
        out_shape=jax.ShapeDtypeStruct((4, 2 * D, PER), BF16),
        in_specs=[spec(pltpu.VMEM)] * 2,
        out_specs=spec(pltpu.VMEM),
        compiler_params=SMALL,
        cost_estimate=pl.CostEstimate(flops=10**7, bytes_accessed=3 * 10**6, transcendentals=0),
    )(q0, q1)


def attend_early(qt, pieces):
    return pl.pallas_call(
        early_kernel,
        name="attend_early",
        out_shape=(RANKS, jax.ShapeDtypeStruct((4, 1, PER), F32)) + STATE,
        in_specs=[spec(pltpu.VMEM)] + [spec(pl.ANY)] * 2,
        out_specs=(spec(pltpu.SMEM),) + (spec(pltpu.VMEM),) * 3,
        scratch_shapes=[pltpu.VMEM((PART + 1, ROWS, D), BF16), *lists(PART), pltpu.SemaphoreType.DMA((2,))],
        compiler_params=PARAMS,
        cost_estimate=cost(PART, 4),
    )(qt, *pieces)


def attend_middle(early_ranks, state, pieces):
    return pl.pallas_call(
        middle_kernel,
        name="attend_middle",
        out_shape=(RANKS,) + STATE,
        in_specs=[spec(pltpu.SMEM)] + [spec(pltpu.VMEM)] * 4 + [spec(pl.ANY)] * 2,
        out_specs=(spec(pltpu.SMEM),) + (spec(pltpu.VMEM),) * 2,
        scratch_shapes=[pltpu.VMEM((PART + 1, ROWS, D), BF16), *lists(PART), pltpu.SemaphoreType.DMA((2,))],
        compiler_params=PARAMS,
        cost_estimate=cost(PART, 4),
    )(early_ranks, *state, *pieces)


def attend_late(ranks, state, pieces, chunk):
    return pl.pallas_call(
        functools.partial(late_kernel, chunk),
        name="attend_late",
        out_shape=(jax.ShapeDtypeStruct((RUN, 4 * D), BF16),) * 2,
        in_specs=[spec(pltpu.SMEM)] * 2 + [spec(pl.ANY)] * 12,
        out_specs=(spec(pltpu.VMEM),) * 2,
        scratch_shapes=[
            pltpu.VMEM((4 * PART + 1, ROWS, D), BF16),
            *held(2),
            pltpu.VMEM((2, 144, PER), F32),
            pltpu.VMEM((2, 8, PER), F32),
            pltpu.SMEM((2 * PART,), I32),
            *lists(2 * PART),
            pltpu.SemaphoreType.DMA((4,)),
            pltpu.SemaphoreType.DMA((4,)),
        ],
        compiler_params=LARGE,
        cost_estimate=cost(2 * PART, 2),
    )(*ranks, *state, *pieces)


def project_kernel(place, even, a0, a1, b0, b1, w_own, w0, w1, w2, w3, out, rows, v_own, v_far, sems):
    width = w0.shape[1]
    copies = []
    for e, w in enumerate((w0, w1, w2, w3)):
        at = pl.ds(pl.multiple_of(place[e] * width, width), width)
        pair = (
            pltpu.make_async_copy(w_own.at[:, at], v_own.at[e], sems.at[2 * e]),
            pltpu.make_async_copy(w, v_far.at[e], sems.at[2 * e + 1]),
        )
        for copy in pair:
            copy.start()
        copies.append(pair)
    half = a0.shape[1]
    for swap in (0, 1):

        @pl.when(even[0] == 1 - swap)
        def _(swap=swap):
            for i, pair in enumerate(((a0, a1), (b0, b1))):
                rows[i, :, 0:half] = pair[swap][...]
                rows[i, :, half : 2 * half] = pair[1 - swap][...]

    for e in range(4):
        for copy in copies[e]:
            copy.wait()
        for j in range(width // SHARE):
            cols = slice(j * SHARE, (j + 1) * SHARE)
            term = jnp.dot(rows[0], v_own[e, :, cols], preferred_element_type=F32)
            term = term + jnp.dot(rows[1], v_far[e, :, cols], preferred_element_type=F32)
            at = pl.ds(pl.multiple_of(place[e] * width + j * SHARE, SHARE), SHARE)
            out[:, at] = term.astype(BF16)


def project(place, even, got, w_own, shares):
    rows, depth = got[0].shape[0], w_own.shape[0]
    width = w_own.shape[1]
    return pl.pallas_call(
        project_kernel,
        name="project",
        out_shape=jax.ShapeDtypeStruct((rows, width), BF16),
        in_specs=[spec(pltpu.SMEM)] * 2 + [spec(pltpu.VMEM)] * 4 + [spec(pl.ANY)] * 5,
        out_specs=spec(pltpu.VMEM),
        scratch_shapes=[
            pltpu.VMEM((2, rows, depth), BF16),
            pltpu.VMEM((4, depth, width // 4), BF16),
            pltpu.VMEM((4, depth, width // 4), BF16),
            pltpu.SemaphoreType.DMA((8,)),
        ],
        compiler_params=LARGE,
        cost_estimate=pl.CostEstimate(
            flops=4 * rows * depth * width, bytes_accessed=20 * 10**6, transcendentals=0
        ),
    )(place, even, *got, w_own, *shares)


def finish_kernel(a, b, *rest):
    rest[-1][...] = (a[...].astype(F32) + b[...].astype(F32)).astype(BF16)


def finish(a, b, chunk, before=None):
    rows, width = a.shape
    whole = pl.BlockSpec((rows // 4, width), lambda i: (i, 0))
    more = {} if before is None else {"input_output_aliases": {2: 0}}
    extra = [] if before is None else [before]
    return pl.pallas_call(
        finish_kernel,
        name="finish",
        grid=(4,),
        out_shape=jax.ShapeDtypeStruct((2 * rows, width), BF16),
        in_specs=[whole, whole] + [spec(pl.ANY)] * len(extra),
        out_specs=pl.BlockSpec((rows // 4, width), lambda i: (4 * chunk + i, 0)),
        compiler_params=SMALL,
        **more,
    )(a, b, *extra)


def body(queries, keys, values, positions, out_weight):
    xl, c = lax.axis_index("xl"), lax.axis_index("c")
    y, z = lax.axis_index("y"), lax.axis_index("z")
    rank = (positions.reshape(2, RUN)[:, 0] // RUN).astype(BF16)
    turned = values.reshape(2, 2, D, D).transpose(0, 1, 3, 2).reshape(2, RUN, D)
    marks = jnp.broadcast_to(rank[:, None, None], (2, 16, D))
    piece = jnp.concatenate([keys.reshape(2, RUN, D), turned, marks], axis=1)
    width = out_weight.shape[1] // 8
    line, bit = jnp.where(c == 0, y, z), jnp.where(c == 0, z, y) % 2
    share = lax.dynamic_slice_in_dim(out_weight, (line * 2 + bit) * width, width, 1)
    piece = route(piece, lambda y, xl, z, xh, c: (y, c, z, xh, xl))
    share = route(share, lambda y, xl, z, xh, c: (y, 1 - xl, z, 1 - xh, c))
    q = []
    for k in (0, 1):
        half = lax.dynamic_slice_in_dim(queries, (xl ^ k) * 4 * D, 4 * D, 1)
        q.append(route(half, lambda y, xl, z, xh, c, k=k: (y, c, z, xh, xl ^ k)))
    near = jnp.concatenate([piece] + [onward(piece, d, 0) for d in SHIFTS[1:]])
    near, q = lax.optimization_barrier((near, q))
    pieces = [near, other_core(near)]
    side = [onward(near, d, 1) for d in SHIFTS[1:]]
    qt = turn(*q)
    ranks, mref, acc, viol = attend_early(qt, pieces)
    side, acc, share = lax.optimization_barrier((side, acc, share))
    other = [other_core(b) for b in side]
    pair = route(share, lambda y, xl, z, xh, c: (y ^ c, xl, z ^ (1 - c), xh, c))
    more, acc, viol = attend_middle(ranks, (qt, mref, acc, viol), side[:2])
    other, acc, share, pair = lax.optimization_barrier((other, acc, share, pair))
    share = jnp.concatenate([jnp.where(bit == 0, share, pair), jnp.where(bit == 0, pair, share)], axis=1)
    shares = [share] + [onward(share, d, 1) for d in (1, 3)]
    pieces = [*pieces, *side, *other]
    place = (line - jnp.array(SHIFTS, I32)) % 4
    even = (xl == 0).astype(I32).reshape(1)
    state = (qt, mref, acc, viol)
    out = None
    for chunk in (0, 1):
        attended = attend_late((ranks, more), state, pieces, chunk)
        got = [
            route(attended[k], lambda y, xl, z, xh, c, k=k, far=far: (y, c ^ k, z, xh ^ far, xl))
            for far in (0, 1)
            for k in (0, 1)
        ]
        if chunk == 0:
            attended, state, shares = lax.optimization_barrier((attended, state, shares))
            shares.append(onward(shares[0], 2, 1))
        part = project(place, even, got, out_weight, shares)
        out = finish(part, other_core(part), chunk, out)
    return out


def solution(mesh):
    fine = Mesh(mesh.devices.reshape(SIZES), AXES)
    tokens, heads = ("y", "xl", "z"), ("xh", "c")
    placed = (P(tokens, heads), P(tokens, heads), P(tokens, heads), P(tokens), P(heads, None))
    return jax.shard_map(body, mesh=fine, in_specs=placed, out_specs=P(tokens, None), check_vma=False)
```

profile of v0, /device:TPU:1, one launch (start us, length us, event | category | flops | bytes accessed | tf_op | source)
XLA Modules:
  0.0 172.0 jit_solution(1427126239645361702)
XLA Ops:
  2.9 4.5 %collective-permute-start = (bf16[2,528,128]{2,1,0:T(8,128)(2,1)S(1)}, bf16[2,528,128]{2,1,0:T(8,128)(2,1)S(1)}, u32[]{:S(2)}, u32[]{:S(2)}) collective-permute-start(bf16[2,528,128]{2,1,0:T(8,128)(2,1)S(1)} %pad_maximum_fusion.2), channel_id=1, source_target_pairs={{0,0},{1,16},{2,2},{3,18},{4,4},{5,20},{6,6},{7,22},{8,8},{9,24},{... | collective-permute-start | bytes 811016 | tf_op jit(solution)/shard_map/ppermute | solution.py:46
  8.7 1.9 %collective-permute-start.4 = (bf16[512,512]{1,0:T(8,128)(2,1)S(1)}, bf16[512,512]{1,0:T(8,128)(2,1)S(1)}, u32[]{:S(2)}, u32[]{:S(2)}) collective-permute-start(bf16[512,512]{1,0:T(8,128)(2,1)S(1)} %get-tuple-element.72), channel_id=1, source_target_pairs={{0,0},{1,16},{2,2},{3,18},{4,4},{5,20},{6,6},{7,22},{8,8},{9,24},{... | collective-permute-start | bytes 1572872 | tf_op jit(solution)/shard_map/ppermute | solution.py:46
  11.5 2.9 %collective-permute-start.3 = (bf16[2,528,128]{2,1,0:T(8,128)(2,1)S(1)}, bf16[2,528,128]{2,1,0:T(8,128)(2,1)S(1)}, u32[]{:S(2)}, u32[]{:S(2)}) collective-permute-start(bf16[2,528,128]{2,1,0:T(8,128)(2,1)S(1)} %collective-permute-done), channel_id=1, source_target_pairs={{0,8},{1,65},{2,10},{3,67},{4,12},{5,69},{6,14},{7,71},{8,0},{9,73... | collective-permute-start | bytes 811016 | tf_op jit(solution)/shard_map/ppermute | solution.py:46
  15.9 2.7 %collective-permute-done.3 = bf16[2,528,128]{2,1,0:T(8,128)(2,1)S(1)} collective-permute-done((bf16[2,528,128]{2,1,0:T(8,128)(2,1)S(1)}, bf16[2,528,128]{2,1,0:T(8,128)(2,1)S(1)}, u32[]{:S(2)}, u32[]{:S(2)}) %collective-permute-start.3) | collective-permute-done | bytes 270368 | tf_op jit(solution)/shard_map/ppermute | solution.py:46
  18.6 3.3 %collective-permute-done.2 = bf16[2,528,128]{2,1,0:T(8,128)(2,1)S(1)} collective-permute-done((bf16[2,528,128]{2,1,0:T(8,128)(2,1)S(1)}, bf16[2,528,128]{2,1,0:T(8,128)(2,1)S(1)}, u32[]{:S(2)}, u32[]{:S(2)}) %collective-permute-start.2) | collective-permute-done | bytes 270368 | tf_op jit(solution)/shard_map/ppermute | solution.py:46
  23.8 2.4 %collective-permute-start.6 = (bf16[8,528,128]{2,1,0:T(8,128)(2,1)S(1)}, bf16[8,528,128]{2,1,0:T(8,128)(2,1)}, u32[]{:S(2)}, u32[]{:S(2)}) collective-permute-start(bf16[8,528,128]{2,1,0:T(8,128)(2,1)S(1)} %pad_maximum_fusion.1.s0.rest_4_), channel_id=1, source_target_pairs={{0,1},{1,0},{2,3},{3,2},{4,5},{5,4},{6,7},{7,6},{8,9},{9,8},{10,11... | collective-permute-start | bytes 3244040 | tf_op jit(solution)/shard_map/ppermute | solution.py:46
  27.9 2.1 %collective-permute-start.8 = (bf16[8,528,128]{2,1,0:T(8,128)(2,1)S(1)}, bf16[8,528,128]{2,1,0:T(8,128)(2,1)}, u32[]{:S(2)}, u32[]{:S(2)}) collective-permute-start(bf16[8,528,128]{2,1,0:T(8,128)(2,1)S(1)} %pad_maximum_fusion.1.s0.rest_4_), channel_id=1, source_target_pairs={{0,96},{1,13},{2,98},{3,15},{4,100},{5,1},{6,102},{7,3},{8,104},{9... | collective-permute-start | bytes 3244040 | tf_op jit(solution)/shard_map/ppermute | solution.py:46
  34.3 15.0 %attend_early.1 = (s32[16]{0:T(128)S(1)}, f32[4,1,1024]{2,1,0:T(1,128)S(1)}, f32[4,144,1024]{2,1,0:T(8,128)S(1)}, f32[4,8,1024]{2,1,0:T(8,128)S(1)}) custom-call(bf16[4,256,1024]{2,1,0:T(8,128)(2,1)S(1)} %turn_queries.1.qt.rest_0_, bf16[8,528,128]{2,1,0:T(8,128)(2,1)S(1)} %pad_maximum_fusion.1.s0.rest_4_, bf16[8,528,128]{2,1,0:T(8,128)(2,1)} %collective-permute-done.6.s1.rest_5_), custom_call_target="tpu_custom_call" | custom-call | flops 8589934592 | bytes 12000000 | tf_op jit(solution)/shard_map/attend_early/pallas_call | solution.py:291
  50.7 7.9 %collective-permute-done.10 = bf16[1024,512]{1,0:T(8,128)(2,1)} collective-permute-done((bf16[1024,512]{1,0:T(8,128)(2,1)S(1)}, bf16[1024,512]{1,0:T(8,128)(2,1)}, u32[]{:S(2)}, u32[]{:S(2)}) %collective-permute-start.10) | collective-permute-done | bytes 1048608 | tf_op jit(solution)/shard_map/ppermute | solution.py:46
  62.6 11.5 %attend_middle.1 = (s32[16]{0:T(128)S(1)}, f32[4,144,1024]{2,1,0:T(8,128)S(1)}, f32[4,8,1024]{2,1,0:T(8,128)S(1)}) custom-call(s32[16]{0:T(128)S(1)} %get-tuple-element.40.early_ranks, bf16[4,256,1024]{2,1,0:T(8,128)(2,1)S(1)} %turn_queries.1.qt.rest_0_, f32[4,1,1024]{2,1,0:T(1,128)S(1)} %get-tuple-element.61.mref.rest_1_, f32[4,144,1024]{2,1,0:T(8,128)S(1)} %copy-done.10, ...), custom_call_target="tpu_custom_call" | custom-call | flops 8589934592 | bytes 12000000 | tf_op jit(solution)/shard_map/attend_middle/pallas_call | solution.py:304
  74.4 2.1 %broadcast_select_fusion.1 = (bf16[1024,512]{1,0:T(8,128)(2,1)S(1)}, bf16[1024,512]{1,0:T(8,128)(2,1)S(1)}) fusion(bf16[1024,512]{1,0:T(8,128)(2,1)} %collective-permute-done.10, bf16[1024,512]{1,0:T(8,128)(2,1)S(1)} %collective-permute-done.14, pred[]{:T(512)S(6)} %eq.17), kind=kLoop, calls=%fused_computation.3 | loop fusion | flops 1048576 | bytes 4194305 | tf_op jit(solution)/shard_map/jit(_where)/select_n | solution.py:440
  76.7 7.6 %collective-permute-start.15 = (bf16[1024,1024]{1,0:T(8,128)(2,1)S(1)}, bf16[1024,1024]{1,0:T(8,128)(2,1)S(1)}, u32[]{:S(2)}, u32[]{:S(2)}) collective-permute-start(bf16[1024,1024]{1,0:T(8,128)(2,1)S(1)} %pad_maximum_fusion.w0), channel_id=1, source_target_pairs={{0,32},{1,5},{2,34},{3,7},{4,36},{5,9},{6,38},{7,11},{8,40},{9,13}... | collective-permute-start | bytes 6291464 | tf_op jit(solution)/shard_map/ppermute | solution.py:46
  84.4 15.8 %attend_late.2 = (bf16[256,512]{1,0:T(8,128)(2,1)}, bf16[256,512]{1,0:T(8,128)(2,1)}) custom-call(s32[16]{0:T(128)} %copy-done.13, s32[16]{0:T(128)} %copy-done.14, bf16[4,256,1024]{2,1,0:T(8,128)(2,1)} %copy-done.2, f32[4,1,1024]{2,1,0:T(1,128)} %copy-done.12, f32[4,144,1024]{2,1,0:T(8,128)} %copy-done.8, f32[4,8,1024]{2,1,0:T(8,128)} %copy-done.11, ...), custom_call_target="tpu_custom_call" | custom-call | flops 8589934592 | bytes 12000000 | tf_op jit(solution)/shard_map/attend_late/pallas_call | solution.py:317
  100.2 7.1 %collective-permute-done.15.w1 = bf16[1024,1024]{1,0:T(8,128)(2,1)S(1)} collective-permute-done((bf16[1024,1024]{1,0:T(8,128)(2,1)S(1)}, bf16[1024,1024]{1,0:T(8,128)(2,1)S(1)}, u32[]{:S(2)}, u32[]{:S(2)}) %collective-permute-start.15) | collective-permute-done | bytes 2097184 | tf_op jit(solution)/shard_map/ppermute | solution.py:46
  116.3 3.1 %collective-permute-start.26 = (bf16[256,512]{1,0:T(8,128)(2,1)}, bf16[256,512]{1,0:T(8,128)(2,1)S(1)}, u32[]{:S(2)}, u32[]{:S(2)}) collective-permute-start(bf16[256,512]{1,0:T(8,128)(2,1)} %get-tuple-element.57), channel_id=1, source_target_pairs={{0,18},{1,2},{2,16},{3,0},{4,22},{5,6},{6,20},{7,4},{8,26},{9,10},... | collective-permute-start | bytes 786440 | tf_op jit(solution)/shard_map/ppermute | solution.py:46
  119.5 17.8 %attend_late.3 = (bf16[256,512]{1,0:T(8,128)(2,1)}, bf16[256,512]{1,0:T(8,128)(2,1)}) custom-call(s32[16]{0:T(128)} %copy-done.13, s32[16]{0:T(128)} %copy-done.14, bf16[4,256,1024]{2,1,0:T(8,128)(2,1)} %copy-done.2, f32[4,1,1024]{2,1,0:T(1,128)} %copy-done.12, f32[4,144,1024]{2,1,0:T(8,128)} %copy-done.8, f32[4,8,1024]{2,1,0:T(8,128)} %copy-done.11, ...), custom_call_target="tpu_custom_call" | custom-call | flops 8589934592 | bytes 12000000 | tf_op jit(solution)/shard_map/attend_late/pallas_call | solution.py:317
  137.3 1.9 %collective-permute-start.17 = (bf16[256,512]{1,0:T(8,128)(2,1)}, bf16[256,512]{1,0:T(8,128)(2,1)S(1)}, u32[]{:S(2)}, u32[]{:S(2)}) collective-permute-start(bf16[256,512]{1,0:T(8,128)(2,1)} %get-tuple-element.64), channel_id=1, source_target_pairs={{0,0},{1,16},{2,2},{3,18},{4,4},{5,20},{6,6},{7,22},{8,8},{9,24},{... | collective-permute-start | bytes 786440 | tf_op jit(solution)/shard_map/ppermute | solution.py:46
  139.2 2.1 %collective-permute-start.19 = (bf16[256,512]{1,0:T(8,128)(2,1)}, bf16[256,512]{1,0:T(8,128)(2,1)S(1)}, u32[]{:S(2)}, u32[]{:S(2)}) collective-permute-start(bf16[256,512]{1,0:T(8,128)(2,1)} %get-tuple-element.64), channel_id=1, source_target_pairs={{0,2},{1,18},{2,0},{3,16},{4,6},{5,22},{6,4},{7,20},{8,10},{9,26},... | collective-permute-start | bytes 786440 | tf_op jit(solution)/shard_map/ppermute | solution.py:46
  141.4 2.4 %collective-permute-start.20 = (bf16[256,512]{1,0:T(8,128)(2,1)}, bf16[256,512]{1,0:T(8,128)(2,1)S(1)}, u32[]{:S(2)}, u32[]{:S(2)}) collective-permute-start(bf16[256,512]{1,0:T(8,128)(2,1)} %get-tuple-element.65), channel_id=1, source_target_pairs={{0,18},{1,2},{2,16},{3,0},{4,22},{5,6},{6,20},{7,4},{8,26},{9,10},... | collective-permute-start | bytes 786440 | tf_op jit(solution)/shard_map/ppermute | solution.py:46
  143.8 10.0 %project.3.a = bf16[256,4096]{1,0:T(8,128)(2,1)} custom-call(s32[4]{0:T(128)} %and_select_fusion.1.place, s32[1]{0:T(128)} %bitcast.even, bf16[256,512]{1,0:T(8,128)(2,1)} %copy-done.18, bf16[256,512]{1,0:T(8,128)(2,1)} %copy-done.19, bf16[256,512]{1,0:T(8,128)(2,1)} %copy-done.20, bf16[256,512]{1,0:T(8,128)(2,1)} %copy-done.22, bf16[1024,4096]{1,0:T(8,128)(2,1)} %w_own.3, ...), custom_call_target="tpu_custom_call" | custom-call | flops 4294967296 | bytes 20000000 | tf_op jit(solution)/shard_map/project/pallas_call | solution.py:373
  155.4 9.9 %project.2.a = bf16[256,4096]{1,0:T(8,128)(2,1)} custom-call(s32[4]{0:T(128)} %and_select_fusion.1.place, s32[1]{0:T(128)} %bitcast.even, bf16[256,512]{1,0:T(8,128)(2,1)} %copy-done.21, bf16[256,512]{1,0:T(8,128)(2,1)} %copy-done.24, bf16[256,512]{1,0:T(8,128)(2,1)} %copy-done.23, bf16[256,512]{1,0:T(8,128)(2,1)} %copy-done.25, bf16[1024,4096]{1,0:T(8,128)(2,1)} %w_own.3, ...), custom_call_target="tpu_custom_call" | custom-call | flops 4294967296 | bytes 20000000 | tf_op jit(solution)/shard_map/project/pallas_call | solution.py:373
  166.0 2.0 %finish.2.rest_0_ = bf16[512,4096]{1,0:T(8,128)(2,1)} custom-call(bf16[256,4096]{1,0:T(8,128)(2,1)S(1)} %copy-done, bf16[256,4096]{1,0:T(8,128)(2,1)S(1)} %collective-permute-done.27.b), custom_call_target="tpu_custom_call" | custom-call | tf_op jit(solution)/shard_map/finish/pallas_call | solution.py:401
  168.0 2.0 %collective-permute-done.22.b = bf16[256,4096]{1,0:T(8,128)(2,1)S(1)} collective-permute-done((bf16[256,4096]{1,0:T(8,128)(2,1)}, bf16[256,4096]{1,0:T(8,128)(2,1)S(1)}, u32[]{:S(2)}, u32[]{:S(2)}) %collective-permute-start.22) | collective-permute-done | bytes 2097184 | tf_op jit(solution)/shard_map/ppermute | solution.py:46
  170.0 2.0 %finish.3 = bf16[512,4096]{1,0:T(8,128)(2,1)} custom-call(bf16[256,4096]{1,0:T(8,128)(2,1)S(1)} %copy-done.1, bf16[256,4096]{1,0:T(8,128)(2,1)S(1)} %collective-permute-done.22.b, bf16[512,4096]{1,0:T(8,128)(2,1)} %finish.2.rest_0_), custom_call_target="tpu_custom_call", output_to_operand_aliasing={{}: (2, {})} | custom-call | tf_op jit(solution)/shard_map/finish/pallas_call | solution.py:401
  (107 shorter events, 31.3 us)
Async XLA Ops:
  2.9 8.6 %collective-permute-start = (bf16[2,528,128]{2,1,0:T(8,128)(2,1)S(1)}, bf16[2,528,128]{2,1,0:T(8,128)(2,1)S(1)}, u32[]{:S(2)}, u32[]{:S(2)}) collective-permute-start(bf16[2,528,128]{2,1,0:T(8,128)(2,1)S(1)} %pad_maximum_fusion.2), channel_id=1, source_target_pairs={{0,0},{1,16},{2,2},{3,18},{4,4},{5,20},{6,6},{7,22},{8,8},{9,24},{... | collective-permute-start | bytes 811016 | tf_op jit(solution)/shard_map/ppermute | solution.py:46
  8.7 13.5 %collective-permute-start.4 = (bf16[512,512]{1,0:T(8,128)(2,1)S(1)}, bf16[512,512]{1,0:T(8,128)(2,1)S(1)}, u32[]{:S(2)}, u32[]{:S(2)}) collective-permute-start(bf16[512,512]{1,0:T(8,128)(2,1)S(1)} %get-tuple-element.72), channel_id=1, source_target_pairs={{0,0},{1,16},{2,2},{3,18},{4,4},{5,20},{6,6},{7,22},{8,8},{9,24},{... | collective-permute-start | bytes 1572872 | tf_op jit(solution)/shard_map/ppermute | solution.py:46
  10.6 12.4 %collective-permute-start.5 = (bf16[512,512]{1,0:T(8,128)(2,1)S(1)}, bf16[512,512]{1,0:T(8,128)(2,1)S(1)}, u32[]{:S(2)}, u32[]{:S(2)}) collective-permute-start(bf16[512,512]{1,0:T(8,128)(2,1)S(1)} %get-tuple-element.71), channel_id=1, source_target_pairs={{0,1},{1,17},{2,3},{3,19},{4,5},{5,21},{6,7},{7,23},{8,9},{9,25},{... | collective-permute-start | bytes 1572872 | tf_op jit(solution)/shard_map/ppermute | solution.py:46
  23.8 10.4 %collective-permute-start.6 = (bf16[8,528,128]{2,1,0:T(8,128)(2,1)S(1)}, bf16[8,528,128]{2,1,0:T(8,128)(2,1)}, u32[]{:S(2)}, u32[]{:S(2)}) collective-permute-start(bf16[8,528,128]{2,1,0:T(8,128)(2,1)S(1)} %pad_maximum_fusion.1.s0.rest_4_), channel_id=1, source_target_pairs={{0,1},{1,0},{2,3},{3,2},{4,5},{5,4},{6,7},{7,6},{8,9},{9,8},{10,11... | collective-permute-start | bytes 3244040 | tf_op jit(solution)/shard_map/ppermute | solution.py:46
  26.3 32.4 %collective-permute-start.7 = (bf16[8,528,128]{2,1,0:T(8,128)(2,1)S(1)}, bf16[8,528,128]{2,1,0:T(8,128)(2,1)}, u32[]{:S(2)}, u32[]{:S(2)}) collective-permute-start(bf16[8,528,128]{2,1,0:T(8,128)(2,1)S(1)} %pad_maximum_fusion.1.s0.rest_4_), channel_id=1, source_target_pairs={{0,32},{1,5},{2,34},{3,7},{4,36},{5,9},{6,38},{7,11},{8,40},{9,13}... | collective-permute-start | bytes 3244040 | tf_op jit(solution)/shard_map/ppermute | solution.py:46
  27.9 30.7 %collective-permute-start.8 = (bf16[8,528,128]{2,1,0:T(8,128)(2,1)S(1)}, bf16[8,528,128]{2,1,0:T(8,128)(2,1)}, u32[]{:S(2)}, u32[]{:S(2)}) collective-permute-start(bf16[8,528,128]{2,1,0:T(8,128)(2,1)S(1)} %pad_maximum_fusion.1.s0.rest_4_), channel_id=1, source_target_pairs={{0,96},{1,13},{2,98},{3,15},{4,100},{5,1},{6,102},{7,3},{8,104},{9... | collective-permute-start | bytes 3244040 | tf_op jit(solution)/shard_map/ppermute | solution.py:46
  30.0 28.6 %collective-permute-start.9 = (bf16[8,528,128]{2,1,0:T(8,128)(2,1)S(1)}, bf16[8,528,128]{2,1,0:T(8,128)(2,1)}, u32[]{:S(2)}, u32[]{:S(2)}) collective-permute-start(bf16[8,528,128]{2,1,0:T(8,128)(2,1)S(1)} %pad_maximum_fusion.1.s0.rest_4_), channel_id=1, source_target_pairs={{0,64},{1,9},{2,66},{3,11},{4,68},{5,13},{6,70},{7,15},{8,72},{9,1... | collective-permute-start | bytes 3244040 | tf_op jit(solution)/shard_map/ppermute | solution.py:46
  32.6 26.0 %collective-permute-start.10 = (bf16[1024,512]{1,0:T(8,128)(2,1)S(1)}, bf16[1024,512]{1,0:T(8,128)(2,1)}, u32[]{:S(2)}, u32[]{:S(2)}) collective-permute-start(bf16[1024,512]{1,0:T(8,128)(2,1)S(1)} %constant_dynamic-slice_fusion), channel_id=1, source_target_pairs={{0,18},{1,19},{2,16},{3,17},{4,22},{5,23},{6,20},{7,21},{8,26},{9,... | collective-permute-start | bytes 3145736 | tf_op jit(solution)/shard_map/ppermute | solution.py:46
  58.7 15.7 %collective-permute-start.11 = (bf16[8,528,128]{2,1,0:T(8,128)(2,1)}, bf16[8,528,128]{2,1,0:T(8,128)(2,1)}, u32[]{:S(2)}, u32[]{:S(2)}) collective-permute-start(bf16[8,528,128]{2,1,0:T(8,128)(2,1)} %collective-permute-done.7.s0.rest_6_), channel_id=1, source_target_pairs={{0,1},{1,0},{2,3},{3,2},{4,5},{5,4},{6,7},{7,6},{8,9},{9,8},{10,11... | collective-permute-start | bytes 3244040 | tf_op jit(solution)/shard_map/ppermute | solution.py:46
  59.7 14.7 %collective-permute-start.12 = (bf16[8,528,128]{2,1,0:T(8,128)(2,1)}, bf16[8,528,128]{2,1,0:T(8,128)(2,1)}, u32[]{:S(2)}, u32[]{:S(2)}) collective-permute-start(bf16[8,528,128]{2,1,0:T(8,128)(2,1)} %collective-permute-done.8.s1.rest_7_), channel_id=1, source_target_pairs={{0,1},{1,0},{2,3},{3,2},{4,5},{5,4},{6,7},{7,6},{8,9},{9,8},{10,11... | collective-permute-start | bytes 3244040 | tf_op jit(solution)/shard_map/ppermute | solution.py:46
  59.8 14.6 %collective-permute-start.13 = (bf16[8,528,128]{2,1,0:T(8,128)(2,1)}, bf16[8,528,128]{2,1,0:T(8,128)(2,1)}, u32[]{:S(2)}, u32[]{:S(2)}) collective-permute-start(bf16[8,528,128]{2,1,0:T(8,128)(2,1)} %collective-permute-done.9.rest_8_), channel_id=1, source_target_pairs={{0,1},{1,0},{2,3},{3,2},{4,5},{5,4},{6,7},{7,6},{8,9},{9,8},{10,11... | collective-permute-start | bytes 3244040 | tf_op jit(solution)/shard_map/ppermute | solution.py:46
  60.2 14.2 %collective-permute-start.14 = (bf16[1024,512]{1,0:T(8,128)(2,1)}, bf16[1024,512]{1,0:T(8,128)(2,1)S(1)}, u32[]{:S(2)}, u32[]{:S(2)}) collective-permute-start(bf16[1024,512]{1,0:T(8,128)(2,1)} %collective-permute-done.10), channel_id=1, source_target_pairs={{0,4},{1,33},{2,6},{3,35},{4,0},{5,37},{6,2},{7,39},{8,12},{9,41},... | collective-permute-start | bytes 3145736 | tf_op jit(solution)/shard_map/ppermute | solution.py:46
  76.7 30.6 %collective-permute-start.15 = (bf16[1024,1024]{1,0:T(8,128)(2,1)S(1)}, bf16[1024,1024]{1,0:T(8,128)(2,1)S(1)}, u32[]{:S(2)}, u32[]{:S(2)}) collective-permute-start(bf16[1024,1024]{1,0:T(8,128)(2,1)S(1)} %pad_maximum_fusion.w0), channel_id=1, source_target_pairs={{0,32},{1,5},{2,34},{3,7},{4,36},{5,9},{6,38},{7,11},{8,40},{9,13}... | collective-permute-start | bytes 6291464 | tf_op jit(solution)/shard_map/ppermute | solution.py:46
  84.4 24.9 %collective-permute-start.16 = (bf16[1024,1024]{1,0:T(8,128)(2,1)S(1)}, bf16[1024,1024]{1,0:T(8,128)(2,1)S(1)}, u32[]{:S(2)}, u32[]{:S(2)}) collective-permute-start(bf16[1024,1024]{1,0:T(8,128)(2,1)S(1)} %pad_maximum_fusion.w0), channel_id=1, source_target_pairs={{0,96},{1,13},{2,98},{3,15},{4,100},{5,1},{6,102},{7,3},{8,104},{9... | collective-permute-start | bytes 6291464 | tf_op jit(solution)/shard_map/ppermute | solution.py:46
  110.6 33.2 %collective-permute-start.21 = (bf16[1024,1024]{1,0:T(8,128)(2,1)S(1)}, bf16[1024,1024]{1,0:T(8,128)(2,1)}, u32[]{:S(2)}, u32[]{:S(2)}) collective-permute-start(bf16[1024,1024]{1,0:T(8,128)(2,1)S(1)} %pad_maximum_fusion.w0), channel_id=1, source_target_pairs={{0,64},{1,9},{2,66},{3,11},{4,68},{5,13},{6,70},{7,15},{8,72},{9,1... | collective-permute-start | bytes 6291464 | tf_op jit(solution)/shard_map/ppermute | solution.py:46
  112.2 25.1 %collective-permute-start.23 = (bf16[256,512]{1,0:T(8,128)(2,1)}, bf16[256,512]{1,0:T(8,128)(2,1)S(1)}, u32[]{:S(2)}, u32[]{:S(2)}) collective-permute-start(bf16[256,512]{1,0:T(8,128)(2,1)} %get-tuple-element.56), channel_id=1, source_target_pairs={{0,0},{1,16},{2,2},{3,18},{4,4},{5,20},{6,6},{7,22},{8,8},{9,24},{... | collective-permute-start | bytes 786440 | tf_op jit(solution)/shard_map/ppermute | solution.py:46
  114.1 25.1 %collective-permute-start.24 = (bf16[256,512]{1,0:T(8,128)(2,1)}, bf16[256,512]{1,0:T(8,128)(2,1)S(1)}, u32[]{:S(2)}, u32[]{:S(2)}) collective-permute-start(bf16[256,512]{1,0:T(8,128)(2,1)} %get-tuple-element.57), channel_id=1, source_target_pairs={{0,16},{1,0},{2,18},{3,2},{4,20},{5,4},{6,22},{7,6},{8,24},{9,8},{... | collective-permute-start | bytes 786440 | tf_op jit(solution)/shard_map/ppermute | solution.py:46
  114.7 26.7 %collective-permute-start.25 = (bf16[256,512]{1,0:T(8,128)(2,1)}, bf16[256,512]{1,0:T(8,128)(2,1)S(1)}, u32[]{:S(2)}, u32[]{:S(2)}) collective-permute-start(bf16[256,512]{1,0:T(8,128)(2,1)} %get-tuple-element.56), channel_id=1, source_target_pairs={{0,2},{1,18},{2,0},{3,16},{4,6},{5,22},{6,4},{7,20},{8,10},{9,26},... | collective-permute-start | bytes 786440 | tf_op jit(solution)/shard_map/ppermute | solution.py:46
  116.3 25.0 %collective-permute-start.26 = (bf16[256,512]{1,0:T(8,128)(2,1)}, bf16[256,512]{1,0:T(8,128)(2,1)S(1)}, u32[]{:S(2)}, u32[]{:S(2)}) collective-permute-start(bf16[256,512]{1,0:T(8,128)(2,1)} %get-tuple-element.57), channel_id=1, source_target_pairs={{0,18},{1,2},{2,16},{3,0},{4,22},{5,6},{6,20},{7,4},{8,26},{9,10},... | collective-permute-start | bytes 786440 | tf_op jit(solution)/shard_map/ppermute | solution.py:46
  137.3 16.6 %collective-permute-start.17 = (bf16[256,512]{1,0:T(8,128)(2,1)}, bf16[256,512]{1,0:T(8,128)(2,1)S(1)}, u32[]{:S(2)}, u32[]{:S(2)}) collective-permute-start(bf16[256,512]{1,0:T(8,128)(2,1)} %get-tuple-element.64), channel_id=1, source_target_pairs={{0,0},{1,16},{2,2},{3,18},{4,4},{5,20},{6,6},{7,22},{8,8},{9,24},{... | collective-permute-start | bytes 786440 | tf_op jit(solution)/shard_map/ppermute | solution.py:46
  139.2 14.7 %collective-permute-start.19 = (bf16[256,512]{1,0:T(8,128)(2,1)}, bf16[256,512]{1,0:T(8,128)(2,1)S(1)}, u32[]{:S(2)}, u32[]{:S(2)}) collective-permute-start(bf16[256,512]{1,0:T(8,128)(2,1)} %get-tuple-element.64), channel_id=1, source_target_pairs={{0,2},{1,18},{2,0},{3,16},{4,6},{5,22},{6,4},{7,20},{8,10},{9,26},... | collective-permute-start | bytes 786440 | tf_op jit(solution)/shard_map/ppermute | solution.py:46
  141.3 12.5 %collective-permute-start.18 = (bf16[256,512]{1,0:T(8,128)(2,1)}, bf16[256,512]{1,0:T(8,128)(2,1)S(1)}, u32[]{:S(2)}, u32[]{:S(2)}) collective-permute-start(bf16[256,512]{1,0:T(8,128)(2,1)} %get-tuple-element.65), channel_id=1, source_target_pairs={{0,16},{1,0},{2,18},{3,2},{4,20},{5,4},{6,22},{7,6},{8,24},{9,8},{... | collective-permute-start | bytes 786440 | tf_op jit(solution)/shard_map/ppermute | solution.py:46
  141.4 12.5 %collective-permute-start.20 = (bf16[256,512]{1,0:T(8,128)(2,1)}, bf16[256,512]{1,0:T(8,128)(2,1)S(1)}, u32[]{:S(2)}, u32[]{:S(2)}) collective-permute-start(bf16[256,512]{1,0:T(8,128)(2,1)} %get-tuple-element.65), channel_id=1, source_target_pairs={{0,18},{1,2},{2,16},{3,0},{4,22},{5,6},{6,20},{7,4},{8,26},{9,10},... | collective-permute-start | bytes 786440 | tf_op jit(solution)/shard_map/ppermute | solution.py:46
  153.8 12.2 %collective-permute-start.27 = (bf16[256,4096]{1,0:T(8,128)(2,1)}, bf16[256,4096]{1,0:T(8,128)(2,1)S(1)}, u32[]{:S(2)}, u32[]{:S(2)}) collective-permute-start(bf16[256,4096]{1,0:T(8,128)(2,1)} %project.3.a), channel_id=1, source_target_pairs={{0,1},{1,0},{2,3},{3,2},{4,5},{5,4},{6,7},{7,6},{8,9},{9,8},{10,11... | collective-permute-start | bytes 6291464 | tf_op jit(solution)/shard_map/ppermute | solution.py:46
  (31 other events, 236.8 us)
where the time goes:
time: 174 us; the launch traced here: 172 us
  Pallas kernels  84.6 us (49%)
  starting transfers between devices  44.7 us (26%)
  waiting for transfers between devices  26.1 us (15%)
  local copies, waits for them, and re-layouts  12.1 us (7%)
  other arithmetic  3.99 us (2%)
    ppermute x28, starting transfers between devices, route(): return lax.ppermute(block, AXES, pairs)  44.7 us
    pallas_call x2, Pallas kernels, attend_late(): pl.pallas_call(functools.partial(late_kernel, chunk), name='attend_late',...  33.6 us
    ppermute x28, waiting for transfers between devices, route(): return lax.ppermute(block, AXES, pairs)  26.1 us
    pallas_call x2, Pallas kernels, project(): pl.pallas_call(project_kernel, name='project', out_shape=jax.ShapeDtypeSt...  19.9 us
    pallas_call x1, Pallas kernels, attend_early(): pl.pallas_call(early_kernel, name='attend_early', out_shape=(RANKS, jax.S...  15 us
    pallas_call x1, Pallas kernels, attend_middle(): pl.pallas_call(middle_kernel, name='attend_middle', out_shape=(RANKS,) +...  11.5 us
    unnamed x54, local copies, waits for them, and re-layouts  7.64 us
    pallas_call x2, Pallas kernels, finish(): pl.pallas_call(finish_kernel, name='finish', grid=(4,), out_shape=jax.Sha...  4 us
  transfers between devices with their start and end apart: 28, of which 9 were waited for; matrix products, arithmetic and copies ran while one was open for 2% of the time, Pallas kernels for 48%

commit v1 on v0

--- a/solution.py
+++ b/solution.py
@@ -66,21 +66,14 @@
     return kv[slot, 0:256, :]
 
 
-def work_list(order, items, ranks, count, rank, run, n):
-    def put(s, found):
-        order[found] = s
-        return found + (ranks[s] < rank).astype(I32)
-
-    found = lax.fori_loop(0, count, put, jnp.int32(0))
-    order[found] = count
-
-    def pair(p, n):
-        items[0, n] = run
-        items[1, n] = order[2 * p]
-        items[2, n] = order[2 * p + 1]
-        return n + 1
-
-    return lax.fori_loop(0, (found + 1) // 2, pair, n)
+def work_list(items, ranks, count, rank, run, n):
+    found = jnp.int32(0)
+    for s in range(count):
+        items[0, n + (found >> 1)] = run
+        items[1 + (found & 1), n + (found >> 1)] = s
+        found = found + (ranks[s] < rank).astype(I32)
+    items[1 + (found & 1), n + (found >> 1)] = count
+    return n + ((found + 1) >> 1)
 
 
 def absorb_items(items, n, kv, base, count, qt, mref, acc, viol):
@@ -114,9 +107,12 @@
             s = later
 
 
-def read_ranks(kv, base, count, ranks):
-    for s in range(count):
-        ranks[s] = jnp.max(kv[base + s, 512:528, :].astype(F32)).astype(I32)
+def read_ranks(copies, kv, base, count, ranks):
+    each = count // len(copies)
+    for i, copy in enumerate(copies):
+        copy.wait()
+        for s in range(i * each, (i + 1) * each):
+            ranks[s] = jnp.max(kv[base + s, 512:528, :].astype(F32)).astype(I32)
 
 
 def fill(kv, base, sources, sems):
@@ -144,13 +140,11 @@
             qt[i, D : 2 * D, here] = (block - high.astype(F32)).astype(BF16)
 
 
-def early_kernel(qt, s0, s1, ranks, mref, acc, viol, kv, order, items, sems):
-    for copy in fill(kv, 0, (s0, s1), sems):
-        copy.wait()
-    read_ranks(kv, 0, PART, ranks)
+def early_kernel(qt, s0, s1, ranks, mref, acc, viol, kv, items, sems):
+    read_ranks(fill(kv, 0, (s0, s1), sems), kv, 0, PART, ranks)
     n = jnp.int32(0)
     for i in range(4):
-        n = work_list(order, items, ranks, PART, ranks[OWN[i]], i, n)
+        n = work_list(items, ranks, PART, ranks[OWN[i]], i, n)
     set_ones(kv, 0, PART)
     kv[PART] = jnp.zeros((ROWS, D), BF16)
     key = lax.broadcasted_iota(I32, (RUN, PER), 0)
@@ -178,16 +172,14 @@
     return copies
 
 
-def middle_kernel(early_ranks, qt, mref, acc_in, viol_in, s0, s1, ranks, acc, viol, kv, order, items, sems):
+def middle_kernel(early_ranks, qt, mref, acc_in, viol_in, s0, s1, ranks, acc, viol, kv, items, sems):
     copies = fill(kv, 0, (s0, s1), sems)
     acc[...] = acc_in[...]
     viol[...] = viol_in[...]
-    for copy in copies:
-        copy.wait()
-    read_ranks(kv, 0, PART, ranks)
+    read_ranks(copies, kv, 0, PART, ranks)
     n = jnp.int32(0)
     for i in range(4):
-        n = work_list(order, items, ranks, PART, early_ranks[OWN[i]], i, n)
+        n = work_list(items, ranks, PART, early_ranks[OWN[i]], i, n)
     set_ones(kv, 0, PART)
     kv[PART] = jnp.zeros((ROWS, D), BF16)
     absorb_items(items, n, kv, 0, PART, qt, mref, acc, viol)
@@ -195,18 +187,18 @@
 
 def late_kernel(chunk, early_ranks, middle_ranks, *rest):
     state, sources = rest[:4], rest[4:12]
-    *out, kv, qt, mref, acc, viol, ranks, order, items, sems, state_sems = rest[12:]
+    *out, kv, qt, mref, acc, viol, ranks, items, sems, state_sems = rest[12:]
     base, count = 2 * PART, 2 * PART
     copies = fill(kv, base, sources[4:], sems)
-    copies += take_state(state, (qt, mref, acc, viol), 2 * chunk, 2, state_sems)
-    for copy in copies:
-        copy.wait()
-    read_ranks(kv, base, count, ranks)
+    state_copies = take_state(state, (qt, mref, acc, viol), 2 * chunk, 2, state_sems)
+    read_ranks(copies, kv, base, count, ranks)
     n = jnp.int32(0)
     for i in range(2):
-        n = work_list(order, items, ranks, count, early_ranks[OWN[2 * chunk + i]], i, n)
+        n = work_list(items, ranks, count, early_ranks[OWN[2 * chunk + i]], i, n)
     set_ones(kv, base, count)
     kv[base + count] = jnp.zeros((ROWS, D), BF16)
+    for copy in state_copies:
+        copy.wait()
     absorb_items(items, n, kv, base, count, qt, mref, acc, viol)
 
     @pl.when(jnp.max(viol[...]) > LIMIT)
@@ -267,12 +259,11 @@
 
 STATE = (jax.ShapeDtypeStruct((4, 144, PER), F32), jax.ShapeDtypeStruct((4, 8, PER), F32))
 PARAMS = pltpu.CompilerParams(vmem_limit_bytes=VMEM)
-LARGE = pltpu.CompilerParams(vmem_limit_bytes=56 * 2**20)
 SMALL = pltpu.CompilerParams(vmem_limit_bytes=12 * 2**20)
 
 
 def lists(slots):
-    return [pltpu.SMEM((slots + 8,), I32), pltpu.SMEM((3, 2 * slots + 16), I32)]
+    return [pltpu.SMEM((3, 2 * slots + 16), I32)]
 
 
 def turn(q0, q1):
@@ -330,23 +321,13 @@
             pltpu.SemaphoreType.DMA((4,)),
             pltpu.SemaphoreType.DMA((4,)),
         ],
-        compiler_params=LARGE,
+        compiler_params=PARAMS,
         cost_estimate=cost(2 * PART, 2),
     )(*ranks, *state, *pieces)
 
 
-def project_kernel(place, even, a0, a1, b0, b1, w_own, w0, w1, w2, w3, out, rows, v_own, v_far, sems):
+def project_kernel(place, even, a0, a1, b0, b1, w_own, w0, w1, w2, w3, out, rows):
     width = w0.shape[1]
-    copies = []
-    for e, w in enumerate((w0, w1, w2, w3)):
-        at = pl.ds(pl.multiple_of(place[e] * width, width), width)
-        pair = (
-            pltpu.make_async_copy(w_own.at[:, at], v_own.at[e], sems.at[2 * e]),
-            pltpu.make_async_copy(w, v_far.at[e], sems.at[2 * e + 1]),
-        )
-        for copy in pair:
-            copy.start()
-        copies.append(pair)
     half = a0.shape[1]
     for swap in (0, 1):
 
@@ -356,14 +337,11 @@
                 rows[i, :, 0:half] = pair[swap][...]
                 rows[i, :, half : 2 * half] = pair[1 - swap][...]
 
-    for e in range(4):
-        for copy in copies[e]:
-            copy.wait()
+    for e, w in enumerate((w0, w1, w2, w3)):
         for j in range(width // SHARE):
-            cols = slice(j * SHARE, (j + 1) * SHARE)
-            term = jnp.dot(rows[0], v_own[e, :, cols], preferred_element_type=F32)
-            term = term + jnp.dot(rows[1], v_far[e, :, cols], preferred_element_type=F32)
             at = pl.ds(pl.multiple_of(place[e] * width + j * SHARE, SHARE), SHARE)
+            term = jnp.dot(rows[0], w_own[:, at], preferred_element_type=F32)
+            term = term + jnp.dot(rows[1], w[:, j * SHARE : (j + 1) * SHARE], preferred_element_type=F32)
             out[:, at] = term.astype(BF16)
 
 
@@ -374,15 +352,10 @@
         project_kernel,
         name="project",
         out_shape=jax.ShapeDtypeStruct((rows, width), BF16),
-        in_specs=[spec(pltpu.SMEM)] * 2 + [spec(pltpu.VMEM)] * 4 + [spec(pl.ANY)] * 5,
+        in_specs=[spec(pltpu.SMEM)] * 2 + [spec(pltpu.VMEM)] * 9,
         out_specs=spec(pltpu.VMEM),
-        scratch_shapes=[
-            pltpu.VMEM((2, rows, depth), BF16),
-            pltpu.VMEM((4, depth, width // 4), BF16),
-            pltpu.VMEM((4, depth, width // 4), BF16),
-            pltpu.SemaphoreType.DMA((8,)),
-        ],
-        compiler_params=LARGE,
+        scratch_shapes=[pltpu.VMEM((2, rows, depth), BF16)],
+        compiler_params=PARAMS,
         cost_estimate=pl.CostEstimate(
             flops=4 * rows * depth * width, bytes_accessed=20 * 10**6, transcendentals=0
         ),

time: 174 us -> 170 us (0.977)
  starting transfers between devices: 44.7 us -> 38.6 us
  local copies, waits for them, and re-layouts: 12.1 us -> 16.7 us
    pallas_call x2, Pallas kernels: 19.9 us -> 13.1 us  [project(): pl.pallas_call(project_kernel, name='project', out_shape=jax.ShapeDtypeSt...]
    ppermute x28, starting transfers between devices: 44.7 us -> 38.6 us  [route(): return lax.ppermute(block, AXES, pairs)]
    pallas_call x1, Pallas kernels: 11.5 us -> 17.4 us  [attend_middle(): pl.pallas_call(middle_kernel, name='attend_middle', out_shape=(RANKS,) +...]
    unnamed x54 -> x42, local copies, waits for them, and re-layouts: 7.64 us -> 12.3 us
    pallas_call x2, Pallas kernels: 33.6 us -> 31.5 us  [attend_late(): pl.pallas_call(functools.partial(late_kernel, chunk), name='attend_late',...]
where the time goes in v1:
time: 170 us; the launch traced here: 168 us
  Pallas kernels  83 us (49%)
  starting transfers between devices  38.6 us (23%)
  waiting for transfers between devices  25.1 us (15%)
  local copies, waits for them, and re-layouts  16.7 us (10%)
  other arithmetic  3.87 us (2%)
    ppermute x28, starting transfers between devices, route(): return lax.ppermute(block, AXES, pairs)  38.6 us
    pallas_call x2, Pallas kernels, attend_late(): pl.pallas_call(functools.partial(late_kernel, chunk), name='attend_late',...  31.5 us
    ppermute x28, waiting for transfers between devices, route(): return lax.ppermute(block, AXES, pairs)  25.1 us
    pallas_call x1, Pallas kernels, attend_middle(): pl.pallas_call(middle_kernel, name='attend_middle', out_shape=(RANKS,) +...  17.4 us
    pallas_call x1, Pallas kernels, attend_early(): pl.pallas_call(early_kernel, name='attend_early', out_shape=(RANKS, jax.S...  16.5 us
    pallas_call x2, Pallas kernels, project(): pl.pallas_call(project_kernel, name='project', out_shape=jax.ShapeDtypeSt...  13.1 us
    unnamed x42, local copies, waits for them, and re-layouts  12.3 us
    pallas_call x2, Pallas kernels, finish(): pl.pallas_call(finish_kernel, name='finish', grid=(4,), out_shape=jax.Sha...  4.03 us
  transfers between devices with their start and end apart: 28, of which 9 were waited for; matrix products, arithmetic and copies ran while one was open for 2% of the time, Pallas kernels for 48%

profile of v1, /device:TPU:1, one launch (start us, length us, event | category | flops | bytes accessed | tf_op | source)
XLA Modules:
  0.0 167.8 jit_solution(13809013466702081673)
XLA Ops:
  2.9 4.5 %collective-permute-start = (bf16[2,528,128]{2,1,0:T(8,128)(2,1)S(1)}, bf16[2,528,128]{2,1,0:T(8,128)(2,1)S(1)}, u32[]{:S(2)}, u32[]{:S(2)}) collective-permute-start(bf16[2,528,128]{2,1,0:T(8,128)(2,1)S(1)} %pad_maximum_fusion.2), channel_id=1, source_target_pairs={{0,0},{1,16},{2,2},{3,18},{4,4},{5,20},{6,6},{7,22},{8,8},{9,24},{... | collective-permute-start | bytes 811016 | tf_op jit(solution)/shard_map/ppermute | solution.py:46
  11.5 2.9 %collective-permute-start.3 = (bf16[2,528,128]{2,1,0:T(8,128)(2,1)S(1)}, bf16[2,528,128]{2,1,0:T(8,128)(2,1)S(1)}, u32[]{:S(2)}, u32[]{:S(2)}) collective-permute-start(bf16[2,528,128]{2,1,0:T(8,128)(2,1)S(1)} %collective-permute-done), channel_id=1, source_target_pairs={{0,8},{1,65},{2,10},{3,67},{4,12},{5,69},{6,14},{7,71},{8,0},{9,73... | collective-permute-start | bytes 811016 | tf_op jit(solution)/shard_map/ppermute | solution.py:46
  15.9 2.7 %collective-permute-done.3 = bf16[2,528,128]{2,1,0:T(8,128)(2,1)S(1)} collective-permute-done((bf16[2,528,128]{2,1,0:T(8,128)(2,1)S(1)}, bf16[2,528,128]{2,1,0:T(8,128)(2,1)S(1)}, u32[]{:S(2)}, u32[]{:S(2)}) %collective-permute-start.3) | collective-permute-done | bytes 270368 | tf_op jit(solution)/shard_map/ppermute | solution.py:46
  18.6 3.3 %collective-permute-done.2 = bf16[2,528,128]{2,1,0:T(8,128)(2,1)S(1)} collective-permute-done((bf16[2,528,128]{2,1,0:T(8,128)(2,1)S(1)}, bf16[2,528,128]{2,1,0:T(8,128)(2,1)S(1)}, u32[]{:S(2)}, u32[]{:S(2)}) %collective-permute-start.2) | collective-permute-done | bytes 270368 | tf_op jit(solution)/shard_map/ppermute | solution.py:46
  23.8 2.5 %collective-permute-start.6 = (bf16[8,528,128]{2,1,0:T(8,128)(2,1)S(1)}, bf16[8,528,128]{2,1,0:T(8,128)(2,1)}, u32[]{:S(2)}, u32[]{:S(2)}) collective-permute-start(bf16[8,528,128]{2,1,0:T(8,128)(2,1)S(1)} %pad_maximum_fusion.1.s0.rest_4_), channel_id=1, source_target_pairs={{0,1},{1,0},{2,3},{3,2},{4,5},{5,4},{6,7},{7,6},{8,9},{9,8},{10,11... | collective-permute-start | bytes 3244040 | tf_op jit(solution)/shard_map/ppermute | solution.py:46
  27.9 2.1 %collective-permute-start.8 = (bf16[8,528,128]{2,1,0:T(8,128)(2,1)S(1)}, bf16[8,528,128]{2,1,0:T(8,128)(2,1)}, u32[]{:S(2)}, u32[]{:S(2)}) collective-permute-start(bf16[8,528,128]{2,1,0:T(8,128)(2,1)S(1)} %pad_maximum_fusion.1.s0.rest_4_), channel_id=1, source_target_pairs={{0,96},{1,13},{2,98},{3,15},{4,100},{5,1},{6,102},{7,3},{8,104},{9... | collective-permute-start | bytes 3244040 | tf_op jit(solution)/shard_map/ppermute | solution.py:46
  34.2 16.5 %attend_early.1 = (s32[16]{0:T(128)S(1)}, f32[4,1,1024]{2,1,0:T(1,128)S(1)}, f32[4,144,1024]{2,1,0:T(8,128)S(1)}, f32[4,8,1024]{2,1,0:T(8,128)S(1)}) custom-call(bf16[4,256,1024]{2,1,0:T(8,128)(2,1)S(1)} %turn_queries.1.qt.rest_0_, bf16[8,528,128]{2,1,0:T(8,128)(2,1)S(1)} %pad_maximum_fusion.1.s0.rest_4_, bf16[8,528,128]{2,1,0:T(8,128)(2,1)} %collective-permute-done.6.s1.rest_5_), custom_call_target="tpu_custom_call" | custom-call | flops 8589934592 | bytes 12000000 | tf_op jit(solution)/shard_map/attend_early/pallas_call | solution.py:282
  52.2 6.5 %collective-permute-done.10 = bf16[1024,512]{1,0:T(8,128)(2,1)} collective-permute-done((bf16[1024,512]{1,0:T(8,128)(2,1)S(1)}, bf16[1024,512]{1,0:T(8,128)(2,1)}, u32[]{:S(2)}, u32[]{:S(2)}) %collective-permute-start.10) | collective-permute-done | bytes 1048608 | tf_op jit(solution)/shard_map/ppermute | solution.py:46
  62.6 17.4 %attend_middle.1 = (s32[16]{0:T(128)S(1)}, f32[4,144,1024]{2,1,0:T(8,128)S(1)}, f32[4,8,1024]{2,1,0:T(8,128)S(1)}) custom-call(s32[16]{0:T(128)S(1)} %get-tuple-element.40.early_ranks, bf16[4,256,1024]{2,1,0:T(8,128)(2,1)S(1)} %turn_queries.1.qt.rest_0_, f32[4,1,1024]{2,1,0:T(1,128)S(1)} %get-tuple-element.61.mref.rest_1_, f32[4,144,1024]{2,1,0:T(8,128)S(1)} %copy-done.15, ...), custom_call_target="tpu_custom_call" | custom-call | flops 8589934592 | bytes 12000000 | tf_op jit(solution)/shard_map/attend_middle/pallas_call | solution.py:295
  80.1 2.5 %broadcast_select_fusion.1 = (bf16[1024,512]{1,0:T(8,128)(2,1)S(1)}, bf16[1024,512]{1,0:T(8,128)(2,1)S(1)}) fusion(bf16[1024,512]{1,0:T(8,128)(2,1)} %collective-permute-done.10, bf16[1024,512]{1,0:T(8,128)(2,1)} %collective-permute-done.14, pred[]{:T(512)S(6)} %eq.17), kind=kLoop, calls=%fused_computation.3 | loop fusion | flops 1048576 | bytes 4194305 | tf_op jit(solution)/shard_map/jit(_where)/select_n | solution.py:413
  83.0 2.7 %collective-permute-start.16 = (bf16[1024,1024]{1,0:T(8,128)(2,1)S(1)}, bf16[1024,1024]{1,0:T(8,128)(2,1)S(1)}, u32[]{:S(2)}, u32[]{:S(2)}) collective-permute-start(bf16[1024,1024]{1,0:T(8,128)(2,1)S(1)} %pad_maximum_fusion.w0), channel_id=1, source_target_pairs={{0,96},{1,13},{2,98},{3,15},{4,100},{5,1},{6,102},{7,3},{8,104},{9... | collective-permute-start | bytes 6291464 | tf_op jit(solution)/shard_map/ppermute | solution.py:46
  85.7 15.7 %attend_late.2 = (bf16[256,512]{1,0:T(8,128)(2,1)S(1)}, bf16[256,512]{1,0:T(8,128)(2,1)S(1)}) custom-call(s32[16]{0:T(128)S(1)} %get-tuple-element.40.early_ranks, s32[16]{0:T(128)S(1)} %get-tuple-element.47.middle_ranks, bf16[4,256,1024]{2,1,0:T(8,128)(2,1)S(1)} %copy-done.5, f32[4,1,1024]{2,1,0:T(1,128)S(1)} %get-tuple-element.61.mref.rest_1_, ...), custom_call_target="tpu_custom_call" | custom-call | flops 8589934592 | bytes 12000000 | tf_op jit(solution)/shard_map/attend_late/pallas_call | solution.py:308
  102.1 6.9 %collective-permute-done.15.w1 = bf16[1024,1024]{1,0:T(8,128)(2,1)S(1)} collective-permute-done((bf16[1024,1024]{1,0:T(8,128)(2,1)S(1)}, bf16[1024,1024]{1,0:T(8,128)(2,1)S(1)}, u32[]{:S(2)}, u32[]{:S(2)}) %collective-permute-start.15) | collective-permute-done | bytes 2097184 | tf_op jit(solution)/shard_map/ppermute | solution.py:46
  111.8 2.3 %collective-permute-start.23 = (bf16[256,512]{1,0:T(8,128)(2,1)}, bf16[256,512]{1,0:T(8,128)(2,1)S(1)}, u32[]{:S(2)}, u32[]{:S(2)}) collective-permute-start(bf16[256,512]{1,0:T(8,128)(2,1)} %copy-done.11), channel_id=1, source_target_pairs={{0,0},{1,16},{2,2},{3,18},{4,4},{5,20},{6,6},{7,22},{8,8},{9,24},{... | collective-permute-start | bytes 786440 | tf_op jit(solution)/shard_map/ppermute | solution.py:46
  116.1 3.2 %collective-permute-start.26 = (bf16[256,512]{1,0:T(8,128)(2,1)S(1)}, bf16[256,512]{1,0:T(8,128)(2,1)S(1)}, u32[]{:S(2)}, u32[]{:S(2)}) collective-permute-start(bf16[256,512]{1,0:T(8,128)(2,1)S(1)} %get-tuple-element.57), channel_id=1, source_target_pairs={{0,18},{1,2},{2,16},{3,0},{4,22},{5,6},{6,20},{7,4},{8,26},{9,10},... | collective-permute-start | bytes 786440 | tf_op jit(solution)/shard_map/ppermute | solution.py:46
  123.5 15.7 %attend_late.3 = (bf16[256,512]{1,0:T(8,128)(2,1)S(1)}, bf16[256,512]{1,0:T(8,128)(2,1)S(1)}) custom-call(s32[16]{0:T(128)S(1)} %get-tuple-element.40.early_ranks, s32[16]{0:T(128)S(1)} %get-tuple-element.47.middle_ranks, bf16[4,256,1024]{2,1,0:T(8,128)(2,1)S(1)} %copy-done.6, f32[4,1,1024]{2,1,0:T(1,128)S(1)} %get-tuple-element.61.mref.rest_1_, ...), custom_call_target="tpu_custom_call" | custom-call | flops 8589934592 | bytes 12000000 | tf_op jit(solution)/shard_map/attend_late/pallas_call | solution.py:308
  141.2 2.0 %collective-permute-start.19 = (bf16[256,512]{1,0:T(8,128)(2,1)S(1)}, bf16[256,512]{1,0:T(8,128)(2,1)S(1)}, u32[]{:S(2)}, u32[]{:S(2)}) collective-permute-start(bf16[256,512]{1,0:T(8,128)(2,1)S(1)} %get-tuple-element.64), channel_id=1, source_target_pairs={{0,2},{1,18},{2,0},{3,16},{4,6},{5,22},{6,4},{7,20},{8,10},{9,26},... | collective-permute-start | bytes 786440 | tf_op jit(solution)/shard_map/ppermute | solution.py:46
  143.2 2.5 %collective-permute-start.20 = (bf16[256,512]{1,0:T(8,128)(2,1)S(1)}, bf16[256,512]{1,0:T(8,128)(2,1)S(1)}, u32[]{:S(2)}, u32[]{:S(2)}) collective-permute-start(bf16[256,512]{1,0:T(8,128)(2,1)S(1)} %get-tuple-element.65), channel_id=1, source_target_pairs={{0,18},{1,2},{2,16},{3,0},{4,22},{5,6},{6,20},{7,4},{8,26},{9,10},... | collective-permute-start | bytes 786440 | tf_op jit(solution)/shard_map/ppermute | solution.py:46
  145.7 6.7 %project.3.a = bf16[256,4096]{1,0:T(8,128)(2,1)S(1)} custom-call(s32[4]{0:T(128)S(1)} %and_select_fusion.1.place, s32[1]{0:T(128)} %bitcast.even, bf16[256,512]{1,0:T(8,128)(2,1)S(1)} %collective-permute-done.23.a0, bf16[256,512]{1,0:T(8,128)(2,1)S(1)} %collective-permute-done.24.a1, bf16[256,512]{1,0:T(8,128)(2,1)S(1)} %collective-permute-done.25.b0, ...), custom_call_target="tpu_custom_call" | custom-call | flops 4294967296 | bytes 20000000 | tf_op jit(solution)/shard_map/project/pallas_call | solution.py:351
  152.5 2.0 %collective-permute-done.19.b0 = bf16[256,512]{1,0:T(8,128)(2,1)S(1)} collective-permute-done((bf16[256,512]{1,0:T(8,128)(2,1)S(1)}, bf16[256,512]{1,0:T(8,128)(2,1)S(1)}, u32[]{:S(2)}, u32[]{:S(2)}) %collective-permute-start.19) | collective-permute-done | bytes 262176 | tf_op jit(solution)/shard_map/ppermute | solution.py:46
  155.1 6.4 %project.2.a = bf16[256,4096]{1,0:T(8,128)(2,1)S(1)} custom-call(s32[4]{0:T(128)S(1)} %and_select_fusion.1.place, s32[1]{0:T(128)} %bitcast.even, bf16[256,512]{1,0:T(8,128)(2,1)S(1)} %collective-permute-done.17.a0, bf16[256,512]{1,0:T(8,128)(2,1)S(1)} %collective-permute-done.18.a1, bf16[256,512]{1,0:T(8,128)(2,1)S(1)} %collective-permute-done.19.b0, ...), custom_call_target="tpu_custom_call" | custom-call | flops 4294967296 | bytes 20000000 | tf_op jit(solution)/shard_map/project/pallas_call | solution.py:351
  161.6 2.0 %finish.2.rest_0_ = bf16[512,4096]{1,0:T(8,128)(2,1)} custom-call(bf16[256,4096]{1,0:T(8,128)(2,1)S(1)} %project.3.a, bf16[256,4096]{1,0:T(8,128)(2,1)S(1)} %collective-permute-done.27.b), custom_call_target="tpu_custom_call" | custom-call | tf_op jit(solution)/shard_map/finish/pallas_call | solution.py:374
  163.7 2.1 %collective-permute-done.22.b = bf16[256,4096]{1,0:T(8,128)(2,1)S(1)} collective-permute-done((bf16[256,4096]{1,0:T(8,128)(2,1)S(1)}, bf16[256,4096]{1,0:T(8,128)(2,1)S(1)}, u32[]{:S(2)}, u32[]{:S(2)}) %collective-permute-start.22) | collective-permute-done | bytes 2097184 | tf_op jit(solution)/shard_map/ppermute | solution.py:46
  165.8 2.0 %finish.3 = bf16[512,4096]{1,0:T(8,128)(2,1)} custom-call(bf16[256,4096]{1,0:T(8,128)(2,1)S(1)} %project.2.a, bf16[256,4096]{1,0:T(8,128)(2,1)S(1)} %collective-permute-done.22.b, bf16[512,4096]{1,0:T(8,128)(2,1)} %finish.2.rest_0_), custom_call_target="tpu_custom_call", output_to_operand_aliasing={{}: (2, {})} | custom-call | tf_op jit(solution)/shard_map/finish/pallas_call | solution.py:374
  (96 shorter events, 34.1 us)
Async XLA Ops:
  2.9 8.6 %collective-permute-start = (bf16[2,528,128]{2,1,0:T(8,128)(2,1)S(1)}, bf16[2,528,128]{2,1,0:T(8,128)(2,1)S(1)}, u32[]{:S(2)}, u32[]{:S(2)}) collective-permute-start(bf16[2,528,128]{2,1,0:T(8,128)(2,1)S(1)} %pad_maximum_fusion.2), channel_id=1, source_target_pairs={{0,0},{1,16},{2,2},{3,18},{4,4},{5,20},{6,6},{7,22},{8,8},{9,24},{... | collective-permute-start | bytes 811016 | tf_op jit(solution)/shard_map/ppermute | solution.py:46
  8.7 13.5 %collective-permute-start.4 = (bf16[512,512]{1,0:T(8,128)(2,1)S(1)}, bf16[512,512]{1,0:T(8,128)(2,1)S(1)}, u32[]{:S(2)}, u32[]{:S(2)}) collective-permute-start(bf16[512,512]{1,0:T(8,128)(2,1)S(1)} %get-tuple-element.72), channel_id=1, source_target_pairs={{0,0},{1,16},{2,2},{3,18},{4,4},{5,20},{6,6},{7,22},{8,8},{9,24},{... | collective-permute-start | bytes 1572872 | tf_op jit(solution)/shard_map/ppermute | solution.py:46
  10.6 12.4 %collective-permute-start.5 = (bf16[512,512]{1,0:T(8,128)(2,1)S(1)}, bf16[512,512]{1,0:T(8,128)(2,1)S(1)}, u32[]{:S(2)}, u32[]{:S(2)}) collective-permute-start(bf16[512,512]{1,0:T(8,128)(2,1)S(1)} %get-tuple-element.71), channel_id=1, source_target_pairs={{0,1},{1,17},{2,3},{3,19},{4,5},{5,21},{6,7},{7,23},{8,9},{9,25},{... | collective-permute-start | bytes 1572872 | tf_op jit(solution)/shard_map/ppermute | solution.py:46
  23.8 10.4 %collective-permute-start.6 = (bf16[8,528,128]{2,1,0:T(8,128)(2,1)S(1)}, bf16[8,528,128]{2,1,0:T(8,128)(2,1)}, u32[]{:S(2)}, u32[]{:S(2)}) collective-permute-start(bf16[8,528,128]{2,1,0:T(8,128)(2,1)S(1)} %pad_maximum_fusion.1.s0.rest_4_), channel_id=1, source_target_pairs={{0,1},{1,0},{2,3},{3,2},{4,5},{5,4},{6,7},{7,6},{8,9},{9,8},{10,11... | collective-permute-start | bytes 3244040 | tf_op jit(solution)/shard_map/ppermute | solution.py:46
  26.3 32.4 %collective-permute-start.7 = (bf16[8,528,128]{2,1,0:T(8,128)(2,1)S(1)}, bf16[8,528,128]{2,1,0:T(8,128)(2,1)}, u32[]{:S(2)}, u32[]{:S(2)}) collective-permute-start(bf16[8,528,128]{2,1,0:T(8,128)(2,1)S(1)} %pad_maximum_fusion.1.s0.rest_4_), channel_id=1, source_target_pairs={{0,32},{1,5},{2,34},{3,7},{4,36},{5,9},{6,38},{7,11},{8,40},{9,13}... | collective-permute-start | bytes 3244040 | tf_op jit(solution)/shard_map/ppermute | solution.py:46
  27.9 30.7 %collective-permute-start.8 = (bf16[8,528,128]{2,1,0:T(8,128)(2,1)S(1)}, bf16[8,528,128]{2,1,0:T(8,128)(2,1)}, u32[]{:S(2)}, u32[]{:S(2)}) collective-permute-start(bf16[8,528,128]{2,1,0:T(8,128)(2,1)S(1)} %pad_maximum_fusion.1.s0.rest_4_), channel_id=1, source_target_pairs={{0,96},{1,13},{2,98},{3,15},{4,100},{5,1},{6,102},{7,3},{8,104},{9... | collective-permute-start | bytes 3244040 | tf_op jit(solution)/shard_map/ppermute | solution.py:46
  30.1 28.6 %collective-permute-start.9 = (bf16[8,528,128]{2,1,0:T(8,128)(2,1)S(1)}, bf16[8,528,128]{2,1,0:T(8,128)(2,1)}, u32[]{:S(2)}, u32[]{:S(2)}) collective-permute-start(bf16[8,528,128]{2,1,0:T(8,128)(2,1)S(1)} %pad_maximum_fusion.1.s0.rest_4_), channel_id=1, source_target_pairs={{0,64},{1,9},{2,66},{3,11},{4,68},{5,13},{6,70},{7,15},{8,72},{9,1... | collective-permute-start | bytes 3244040 | tf_op jit(solution)/shard_map/ppermute | solution.py:46
  32.7 26.0 %collective-permute-start.10 = (bf16[1024,512]{1,0:T(8,128)(2,1)S(1)}, bf16[1024,512]{1,0:T(8,128)(2,1)}, u32[]{:S(2)}, u32[]{:S(2)}) collective-permute-start(bf16[1024,512]{1,0:T(8,128)(2,1)S(1)} %constant_dynamic-slice_fusion), channel_id=1, source_target_pairs={{0,18},{1,19},{2,16},{3,17},{4,22},{5,23},{6,20},{7,21},{8,26},{9,... | collective-permute-start | bytes 3145736 | tf_op jit(solution)/shard_map/ppermute | solution.py:46
  58.7 21.4 %collective-permute-start.11 = (bf16[8,528,128]{2,1,0:T(8,128)(2,1)}, bf16[8,528,128]{2,1,0:T(8,128)(2,1)}, u32[]{:S(2)}, u32[]{:S(2)}) collective-permute-start(bf16[8,528,128]{2,1,0:T(8,128)(2,1)} %collective-permute-done.7.s0.rest_6_), channel_id=1, source_target_pairs={{0,1},{1,0},{2,3},{3,2},{4,5},{5,4},{6,7},{7,6},{8,9},{9,8},{10,11... | collective-permute-start | bytes 3244040 | tf_op jit(solution)/shard_map/ppermute | solution.py:46
  59.7 20.4 %collective-permute-start.12 = (bf16[8,528,128]{2,1,0:T(8,128)(2,1)}, bf16[8,528,128]{2,1,0:T(8,128)(2,1)}, u32[]{:S(2)}, u32[]{:S(2)}) collective-permute-start(bf16[8,528,128]{2,1,0:T(8,128)(2,1)} %collective-permute-done.8.s1.rest_7_), channel_id=1, source_target_pairs={{0,1},{1,0},{2,3},{3,2},{4,5},{5,4},{6,7},{7,6},{8,9},{9,8},{10,11... | collective-permute-start | bytes 3244040 | tf_op jit(solution)/shard_map/ppermute | solution.py:46
  59.8 20.3 %collective-permute-start.13 = (bf16[8,528,128]{2,1,0:T(8,128)(2,1)}, bf16[8,528,128]{2,1,0:T(8,128)(2,1)}, u32[]{:S(2)}, u32[]{:S(2)}) collective-permute-start(bf16[8,528,128]{2,1,0:T(8,128)(2,1)} %collective-permute-done.9.rest_8_), channel_id=1, source_target_pairs={{0,1},{1,0},{2,3},{3,2},{4,5},{5,4},{6,7},{7,6},{8,9},{9,8},{10,11... | collective-permute-start | bytes 3244040 | tf_op jit(solution)/shard_map/ppermute | solution.py:46
  60.2 19.8 %collective-permute-start.14 = (bf16[1024,512]{1,0:T(8,128)(2,1)}, bf16[1024,512]{1,0:T(8,128)(2,1)}, u32[]{:S(2)}, u32[]{:S(2)}) collective-permute-start(bf16[1024,512]{1,0:T(8,128)(2,1)} %collective-permute-done.10), channel_id=1, source_target_pairs={{0,4},{1,33},{2,6},{3,35},{4,0},{5,37},{6,2},{7,39},{8,12},{9,41},... | collective-permute-start | bytes 3145736 | tf_op jit(solution)/shard_map/ppermute | solution.py:46
  82.9 26.2 %collective-permute-start.15 = (bf16[1024,1024]{1,0:T(8,128)(2,1)S(1)}, bf16[1024,1024]{1,0:T(8,128)(2,1)S(1)}, u32[]{:S(2)}, u32[]{:S(2)}) collective-permute-start(bf16[1024,1024]{1,0:T(8,128)(2,1)S(1)} %pad_maximum_fusion.w0), channel_id=1, source_target_pairs={{0,32},{1,5},{2,34},{3,7},{4,36},{5,9},{6,38},{7,11},{8,40},{9,13}... | collective-permute-start | bytes 6291464 | tf_op jit(solution)/shard_map/ppermute | solution.py:46
  83.0 27.4 %collective-permute-start.16 = (bf16[1024,1024]{1,0:T(8,128)(2,1)S(1)}, bf16[1024,1024]{1,0:T(8,128)(2,1)S(1)}, u32[]{:S(2)}, u32[]{:S(2)}) collective-permute-start(bf16[1024,1024]{1,0:T(8,128)(2,1)S(1)} %pad_maximum_fusion.w0), channel_id=1, source_target_pairs={{0,96},{1,13},{2,98},{3,15},{4,100},{5,1},{6,102},{7,3},{8,104},{9... | collective-permute-start | bytes 6291464 | tf_op jit(solution)/shard_map/ppermute | solution.py:46
  111.8 33.9 %collective-permute-start.21 = (bf16[1024,1024]{1,0:T(8,128)(2,1)S(1)}, bf16[1024,1024]{1,0:T(8,128)(2,1)}, u32[]{:S(2)}, u32[]{:S(2)}) collective-permute-start(bf16[1024,1024]{1,0:T(8,128)(2,1)S(1)} %pad_maximum_fusion.w0), channel_id=1, source_target_pairs={{0,64},{1,9},{2,66},{3,11},{4,68},{5,13},{6,70},{7,15},{8,72},{9,1... | collective-permute-start | bytes 6291464 | tf_op jit(solution)/shard_map/ppermute | solution.py:46
  111.8 27.4 %collective-permute-start.23 = (bf16[256,512]{1,0:T(8,128)(2,1)}, bf16[256,512]{1,0:T(8,128)(2,1)S(1)}, u32[]{:S(2)}, u32[]{:S(2)}) collective-permute-start(bf16[256,512]{1,0:T(8,128)(2,1)} %copy-done.11), channel_id=1, source_target_pairs={{0,0},{1,16},{2,2},{3,18},{4,4},{5,20},{6,6},{7,22},{8,8},{9,24},{... | collective-permute-start | bytes 786440 | tf_op jit(solution)/shard_map/ppermute | solution.py:46
  114.1 27.0 %collective-permute-start.24 = (bf16[256,512]{1,0:T(8,128)(2,1)S(1)}, bf16[256,512]{1,0:T(8,128)(2,1)S(1)}, u32[]{:S(2)}, u32[]{:S(2)}) collective-permute-start(bf16[256,512]{1,0:T(8,128)(2,1)S(1)} %get-tuple-element.57), channel_id=1, source_target_pairs={{0,16},{1,0},{2,18},{3,2},{4,20},{5,4},{6,22},{7,6},{8,24},{9,8},{... | collective-permute-start | bytes 786440 | tf_op jit(solution)/shard_map/ppermute | solution.py:46
  114.2 29.0 %collective-permute-start.25 = (bf16[256,512]{1,0:T(8,128)(2,1)}, bf16[256,512]{1,0:T(8,128)(2,1)S(1)}, u32[]{:S(2)}, u32[]{:S(2)}) collective-permute-start(bf16[256,512]{1,0:T(8,128)(2,1)} %copy-done.11), channel_id=1, source_target_pairs={{0,2},{1,18},{2,0},{3,16},{4,6},{5,22},{6,4},{7,20},{8,10},{9,26},... | collective-permute-start | bytes 786440 | tf_op jit(solution)/shard_map/ppermute | solution.py:46
  116.1 27.1 %collective-permute-start.26 = (bf16[256,512]{1,0:T(8,128)(2,1)S(1)}, bf16[256,512]{1,0:T(8,128)(2,1)S(1)}, u32[]{:S(2)}, u32[]{:S(2)}) collective-permute-start(bf16[256,512]{1,0:T(8,128)(2,1)S(1)} %get-tuple-element.57), channel_id=1, source_target_pairs={{0,18},{1,2},{2,16},{3,0},{4,22},{5,6},{6,20},{7,4},{8,26},{9,10},... | collective-permute-start | bytes 786440 | tf_op jit(solution)/shard_map/ppermute | solution.py:46
  139.2 13.2 %collective-permute-start.17 = (bf16[256,512]{1,0:T(8,128)(2,1)S(1)}, bf16[256,512]{1,0:T(8,128)(2,1)S(1)}, u32[]{:S(2)}, u32[]{:S(2)}) collective-permute-start(bf16[256,512]{1,0:T(8,128)(2,1)S(1)} %get-tuple-element.64), channel_id=1, source_target_pairs={{0,0},{1,16},{2,2},{3,18},{4,4},{5,20},{6,6},{7,22},{8,8},{9,24},{... | collective-permute-start | bytes 786440 | tf_op jit(solution)/shard_map/ppermute | solution.py:46
  141.2 13.3 %collective-permute-start.19 = (bf16[256,512]{1,0:T(8,128)(2,1)S(1)}, bf16[256,512]{1,0:T(8,128)(2,1)S(1)}, u32[]{:S(2)}, u32[]{:S(2)}) collective-permute-start(bf16[256,512]{1,0:T(8,128)(2,1)S(1)} %get-tuple-element.64), channel_id=1, source_target_pairs={{0,2},{1,18},{2,0},{3,16},{4,6},{5,22},{6,4},{7,20},{8,10},{9,26},... | collective-permute-start | bytes 786440 | tf_op jit(solution)/shard_map/ppermute | solution.py:46
  143.2 9.3 %collective-permute-start.18 = (bf16[256,512]{1,0:T(8,128)(2,1)S(1)}, bf16[256,512]{1,0:T(8,128)(2,1)S(1)}, u32[]{:S(2)}, u32[]{:S(2)}) collective-permute-start(bf16[256,512]{1,0:T(8,128)(2,1)S(1)} %get-tuple-element.65), channel_id=1, source_target_pairs={{0,16},{1,0},{2,18},{3,2},{4,20},{5,4},{6,22},{7,6},{8,24},{9,8},{... | collective-permute-start | bytes 786440 | tf_op jit(solution)/shard_map/ppermute | solution.py:46
  143.2 11.9 %collective-permute-start.20 = (bf16[256,512]{1,0:T(8,128)(2,1)S(1)}, bf16[256,512]{1,0:T(8,128)(2,1)S(1)}, u32[]{:S(2)}, u32[]{:S(2)}) collective-permute-start(bf16[256,512]{1,0:T(8,128)(2,1)S(1)} %get-tuple-element.65), channel_id=1, source_target_pairs={{0,18},{1,2},{2,16},{3,0},{4,22},{5,6},{6,20},{7,4},{8,26},{9,10},... | collective-permute-start | bytes 786440 | tf_op jit(solution)/shard_map/ppermute | solution.py:46
  152.4 9.3 %collective-permute-start.27 = (bf16[256,4096]{1,0:T(8,128)(2,1)S(1)}, bf16[256,4096]{1,0:T(8,128)(2,1)S(1)}, u32[]{:S(2)}, u32[]{:S(2)}) collective-permute-start(bf16[256,4096]{1,0:T(8,128)(2,1)S(1)} %project.3.a), channel_id=1, source_target_pairs={{0,1},{1,0},{2,3},{3,2},{4,5},{5,4},{6,7},{7,6},{8,9},{9,8},{10,11... | collective-permute-start | bytes 6291464 | tf_op jit(solution)/shard_map/ppermute | solution.py:46
  (25 other events, 255.5 us)
